TPU v7x, 32 devices: a whole 2x2x4 slice. The times are simulated.
32 devices in a mesh: groups: 2 (over x), dev: 16 (over z, y, core).
Axes of the slice: x: 2, y: 2, z: 4, core: 2. Of those that a mesh axis runs over, the one named last changes fastest.
Arguments:
- hidden: bfloat16 [64, 384, 4608], P(('groups', 'dev')), parts along dimension 0, may hold values from -6 to 6
- norm_gain: bfloat16 [4608], replicated, may hold values from 0.099609375 to 1.8984375
- w_key: bfloat16 [4608, 1024], P('dev'), may hold values from -0.09375 to 0.09375
- w_value: bfloat16 [4608, 1024], P('dev'), may hold values from -0.09375 to 0.09375
- queries: bfloat16 [32, 4, 2048], P(('groups', 'dev')), parts along dimension 0, may hold values from -174 to 174
- new_keys: bfloat16 [32, 4, 1024], P(('groups', 'dev')), parts along dimension 0, may hold values from -6 to 6
- new_values: bfloat16 [32, 4, 1024], P(('groups', 'dev')), parts along dimension 0, may hold values from -6 to 6
- passage_owner: int32 [64], P('groups'), parts along dimension 0, may hold values from 0 to 15, as said below
Outputs:
- attended: bfloat16 [32, 4, 2048], P(('groups', 'dev')), parts along dimension 0
There are 2 independent parts, one for each index of `groups`. A program takes and returns all parts, laid end to end along the dimension named above; an argument that names none is the same for every part. Nothing has to cross between parts.
Inputs may be any that keep to these rules, and one draw needn't show every extreme that they name: Passage p lies on device p // 2 and belongs to the request owned by device passage_owner[p], which lies at most 1 positions from that device along dev, counted cyclically; in each direction some passage lies exactly 1 away.
All inputs are finite; a program needn't handle non-finite values.
Results may differ from a plain program's by a relative error of at most 0.0049.
Values may be sent and summed in bfloat16 or wider, within the bound.
A program may use at most 128 MiB of HBM per device.

v0:
```python
import jax
import jax.numpy as jnp
from jax import lax
from jax.sharding import PartitionSpec as P

HEAD_DIM = 128
KV_HEADS = 8
Q_HEADS = 16
STEPS = 4


CAP_LIMIT = 50.0
QUERY_SCALE = 1.0 / 12.0
EPSILON = 1e-06


def passed_along(block, axis, distance):
    devices = range(lax.axis_size(axis))
    route = [((i - distance) % len(devices), i) for i in devices]
    return lax.ppermute(block, axis, route)


def rotate_keys(raw_keys, head_count, head_width):
    length = raw_keys.shape[0]
    half_width = head_width // 2
    blocked = raw_keys.reshape(length, head_count, head_width)
    position = jnp.arange(length, dtype=jnp.float32)
    inverse = 10000.0 ** (-(jnp.arange(half_width, dtype=jnp.float32) * 2.0) / head_width)
    angles = position[:, None] * inverse[None, :]
    cosine = jnp.cos(angles)[:, None, :]
    sine_part = jnp.sin(angles)[:, None, :]
    lower_half = blocked[:, :, :half_width]
    upper_half = blocked[:, :, half_width:]
    turned = jnp.concatenate(
        [
            lower_half * cosine - upper_half * sine_part,
            upper_half * cosine + lower_half * sine_part,
        ],
        axis=-1,
    )
    return turned.reshape(length, head_count * head_width)


def rotate_passage(raw_passage):
    return rotate_keys(raw_passage, KV_HEADS, HEAD_DIM)


def softcap_exp(scores):
    return jnp.exp(CAP_LIMIT * jnp.tanh(scores * QUERY_SCALE / CAP_LIMIT))


def capped_weights(grouped, key_rows):
    scores = jnp.einsum("sghd,kgd->sghk", grouped, key_rows, preferred_element_type=jnp.float32)
    return softcap_exp(scores)


def passage_pairs(grouped_each, key_blocks, value_blocks):
    key_rows = key_blocks.reshape(key_blocks.shape[0], key_blocks.shape[1], KV_HEADS, HEAD_DIM)
    value_rows = value_blocks.reshape(
        value_blocks.shape[0], value_blocks.shape[1], KV_HEADS, HEAD_DIM
    )
    scores = jnp.einsum(
        "psghd,pkgd->psghk", grouped_each, key_rows, preferred_element_type=jnp.float32
    )
    weights = softcap_exp(scores)
    rounded = weights.astype(jnp.bfloat16)
    numerator = jnp.einsum(
        "psghk,pkgd->psghd", rounded, value_rows, preferred_element_type=jnp.float32
    )
    return (numerator, jnp.sum(weights, axis=-1))


def add_flagged(numerator, denominator, chosen, part_num, part_den):
    weight_flag = chosen.astype(jnp.float32)
    numerator = numerator + jnp.sum(weight_flag[:, None, None, None, None] * part_num, axis=0)
    denominator = denominator + jnp.sum(weight_flag[:, None, None, None] * part_den, axis=0)
    return (numerator, denominator)


def group_queries(query_rows):
    return query_rows.reshape(
        query_rows.shape[:-2] + (STEPS, KV_HEADS, Q_HEADS // KV_HEADS, HEAD_DIM)
    )


def shards(hidden, norm_gain, w_key, w_value, queries, new_keys, new_values, passage_owner):
    passage_count = hidden.shape[0]
    pass_length = hidden.shape[1]
    model_width = hidden.shape[2]
    flat_rows = hidden.reshape(passage_count * pass_length, model_width)
    values32 = flat_rows.astype(jnp.float32)
    mean_square = jnp.mean(values32 * values32, axis=-1, keepdims=True)
    normed = (values32 * lax.rsqrt(mean_square + EPSILON) * norm_gain.astype(jnp.float32)).astype(
        jnp.bfloat16
    )
    key_part = jnp.dot(
        normed, lax.all_gather(w_key, "dev", axis=0, tiled=True), preferred_element_type=jnp.float32
    )
    value_part = jnp.dot(
        normed,
        lax.all_gather(w_value, "dev", axis=0, tiled=True),
        preferred_element_type=jnp.float32,
    )
    turned = jax.vmap(rotate_passage)(key_part.reshape(passage_count, pass_length, -1))
    cache_keys = turned.astype(jnp.bfloat16)
    cache_values = value_part.reshape(passage_count, pass_length, -1).astype(jnp.bfloat16)
    device_count = lax.axis_size("dev")
    myself = lax.axis_index("dev")

    def owners_of(device):
        return lax.dynamic_slice_in_dim(passage_owner, device * passage_count, passage_count)

    my_owners = owners_of(myself)
    grouped = group_queries(queries[0])
    fresh_weights = capped_weights(grouped, new_keys[0].reshape(STEPS, KV_HEADS, HEAD_DIM))
    causal = jnp.arange(STEPS)[:, None] >= jnp.arange(STEPS)[None, :]
    fresh_weights = jnp.where(causal[:, None, None, :], fresh_weights, jnp.float32(0.0))
    fresh_vals = new_values[0].reshape(STEPS, KV_HEADS, HEAD_DIM)
    numerator = jnp.einsum(
        "sghk,kgd->sghd",
        fresh_weights.astype(jnp.bfloat16),
        fresh_vals,
        preferred_element_type=jnp.float32,
    )
    denominator = jnp.sum(fresh_weights, axis=-1)
    offsets = [1] + [-1]
    own_queries = queries[0]
    selected = jnp.broadcast_to(own_queries[None], (passage_count,) + own_queries.shape)
    for offset in offsets:
        got_queries = passed_along(own_queries, "dev", -offset)
        matches = (myself + offset) % device_count == my_owners
        selected = jnp.where(matches[:, None, None], got_queries[None], selected)
    part_num, part_den = passage_pairs(group_queries(selected), cache_keys, cache_values)
    numerator, denominator = add_flagged(
        numerator, denominator, my_owners == myself, part_num, part_den
    )
    for offset in offsets:
        got_num, got_den = passed_along((part_num, part_den), "dev", offset)
        source = (myself - offset) % device_count
        numerator, denominator = add_flagged(
            numerator, denominator, owners_of(source) == myself, got_num, got_den
        )
    result = numerator / denominator[..., None]
    return result.reshape(1, STEPS, Q_HEADS * HEAD_DIM).astype(jnp.bfloat16)


def solution(mesh):
    return jax.shard_map(
        shards,
        mesh=mesh,
        in_specs=(
            P(("groups", "dev"), None, None),
            P(),
            P("dev", None),
            P("dev", None),
            P(("groups", "dev"), None, None),
            P(("groups", "dev"), None, None),
            P(("groups", "dev"), None, None),
            P("groups"),
        ),
        out_specs=P(("groups", "dev"), None, None),
        check_vma=False,
    )
```

profile of v0, /device:TPU:0, one launch (start us, length us, event | category | flops | bytes accessed | tf_op | source)
XLA Modules:
  0.0 203.4 jit_solution(11013796725495332950)
XLA Ops:
  6.5 0.7 all-gather.5.cloned.1.call-update
  7.3 0.7 all-gather.3.cloned.1.call-update
  8.0 0.5 collective-permute-start
  8.5 5.1 %collective-permute-start.1 = (bf16[4,2048]{1,0:T(4,128)(2,1)}, bf16[4,2048]{1,0:T(4,128)(2,1)S(1)}, u32[]{:S(2)}, u32[]{:S(2)}) collective-permute-start(bf16[4,2048]{1,0:T(4,128)(2,1)} %bitcast.99), channel_id=1, source_target_pairs={{1,0},{2,1},{3,2},{4,3},{5,4},{6,5},{7,6},{8,7},{9,8},{10,9},{11,1... | collective-permute-start | bytes 49160 | tf_op jit(solution)/shard_map/ppermute | solution.py:20
  13.6 0.7 convert_element_type.51
  14.3 0.9 fusion.40
  15.4 0.1 copy.55
  15.6 0.9 compare_convert_fusion.2
  16.4 4.5 %fusion = f32[2,384]{1,0:T(2,128)S(1)} fusion(bf16[2,384,4608]{2,1,0:T(8,128)(2,1)} %param.8), kind=kLoop, calls=%fused_computation.2 | loop fusion | flops 10616064 | bytes 7080960 | tf_op jit(solution)/shard_map/reduce_sum | solution.py:92
  20.9 0.4 fusion.32
  21.3 72.5 %all-gather.5.cloned.1.call-done = bf16[4608,1024]{1,0:T(8,128)(2,1)} async-done(((bf16[288,1024]{1,0:T(8,128)(2,1)}), bf16[4608,1024]{1,0:T(8,128)(2,1)}) %all-gather.5.cloned.1.call-update) | async-done | bytes 9437200 | tf_op jit(solution)/shard_map/all_gather | solution.py:97
  93.8 12.8 %copy.57 = bf16[1024,4608]{1,0:T(8,128)(2,1)} copy(bf16[1024,4608]{0,1:T(8,128)(2,1)} %bitcast.89) | data formatting | bytes 18874368 | tf_op jit(solution)/shard_map/dot_general | solution.py:96
  106.6 11.5 %fusion.5 = f32[2,384,8,128]{1,3,2,0:T(8,128)S(1)} fusion(bf16[8,128,4608,1]{2,1,0,3:T(8,128)(2,1)} %bitcast.90, bf16[2,384,4608]{2,1,0:T(8,128)(2,1)} %param.8, f32[4608]{0:T(1024)S(1)} %convert_element_type.51, f32[2,384]{1,0:T(2,128)S(1)} %add_rsqrt_fusion), kind=kOutput, calls=%fused_computation.7 | convolution fusion | flops 7261913088 | bytes 19682304 | tf_op jit(solution)/shard_map/dot_general | solution.py:96
  118.1 0.5 subtract_convert_fusion
  118.6 0.6 fusion.47
  119.2 1.4 collective-permute-start.5
  120.6 55.3 %all-gather.3.cloned.1.call-done = bf16[4608,1024]{1,0:T(8,128)(2,1)} async-done(((bf16[288,1024]{1,0:T(8,128)(2,1)}), bf16[4608,1024]{1,0:T(8,128)(2,1)}) %all-gather.3.cloned.1.call-update) | async-done | bytes 9437200 | tf_op jit(solution)/shard_map/all_gather | solution.py:101
  175.9 12.2 %fusion.9 = bf16[2,384,1024]{2,1,0:T(8,128)(2,1)S(1)} fusion(bf16[4608,1024]{1,0:T(8,128)(2,1)} %all-gather.3.cloned.1.call-done, bf16[2,384,4608]{2,1,0:T(8,128)(2,1)} %param.8, f32[4608]{0:T(1024)S(1)} %convert_element_type.51, f32[2,384]{1,0:T(2,128)S(1)} %add_rsqrt_fusion), kind=kOutput, calls=%fused_computation.9 | convolution fusion | flops 7262699520 | bytes 18109440 | tf_op jit(solution)/shard_map/dot_general | solution.py:99
  188.1 0.4 copy.79
  188.7 0.4 multiply_reduce_fusion.2
  189.2 0.3 collective-permute-start.2
  189.5 4.2 %collective-permute-start.3 = (f32[2,4,8,2,128]{4,1,3,2,0:T(4,128)S(1)}, f32[2,4,8,2,128]{4,1,3,2,0:T(4,128)S(1)}, u32[]{:S(2)}, u32[]{:S(2)}) collective-permute-start(f32[2,4,8,2,128]{4,1,3,2,0:T(4,128)S(1)} %get-tuple-element.17), channel_id=1, source_target_pairs={{1,0},{2,1},{3,2},{4,3},{5,4},{6,5},{7,6},{8,7},{9,8},{10,9},{11,1... | collective-permute-start | bytes 196616 | tf_op jit(solution)/shard_map/ppermute | solution.py:20
  194.2 1.4 collective-permute-done.2
  195.8 0.7 fusion.29
  (28 shorter events, 1.2 us)
Async XLA Ops:
  6.5 189.3 %copy-start = (bf16[1,4,1024]{2,1,0:T(4,128)(2,1)S(1)}, bf16[1,4,1024]{2,1,0:T(4,128)(2,1)}, u32[]{:S(2)}) copy-start(bf16[1,4,1024]{2,1,0:T(4,128)(2,1)} %param.14) | copy-start | bytes 24580
  6.5 87.3 %all-gather.5.cloned.1.call-start = ((), (), s32[]{:S(2)}) async-start(), calls=%async_computation.1 | async-start | bytes 10027008 | tf_op jit(solution)/shard_map/all_gather | solution.py:97
  7.3 168.6 %all-gather.3.cloned.1.call-start = ((), (), s32[]{:S(2)}) async-start(), calls=%async_computation | async-start | bytes 10027008 | tf_op jit(solution)/shard_map/all_gather | solution.py:101
  8.0 110.6 %collective-permute-start = (bf16[4,2048]{1,0:T(4,128)(2,1)}, bf16[4,2048]{1,0:T(4,128)(2,1)S(1)}, u32[]{:S(2)}, u32[]{:S(2)}) collective-permute-start(bf16[4,2048]{1,0:T(4,128)(2,1)} %bitcast.98), channel_id=1, source_target_pairs={{15,0},{0,1},{1,2},{2,3},{3,4},{4,5},{5,6},{6,7},{7,8},{8,9},{9,10... | collective-permute-start | bytes 49160 | tf_op jit(solution)/shard_map/ppermute | solution.py:20
  8.5 110.1 %collective-permute-start.1 = (bf16[4,2048]{1,0:T(4,128)(2,1)}, bf16[4,2048]{1,0:T(4,128)(2,1)S(1)}, u32[]{:S(2)}, u32[]{:S(2)}) collective-permute-start(bf16[4,2048]{1,0:T(4,128)(2,1)} %bitcast.99), channel_id=1, source_target_pairs={{1,0},{2,1},{3,2},{4,3},{5,4},{6,5},{7,6},{8,7},{9,8},{10,9},{11,1... | collective-permute-start | bytes 49160 | tf_op jit(solution)/shard_map/ppermute | solution.py:20
  106.6 12.0 %copy-start.1 = (bf16[1,4,2048]{2,1,0:T(4,128)(2,1)S(1)}, bf16[1,4,2048]{2,1,0:T(4,128)(2,1)}, u32[]{:S(2)}) copy-start(bf16[1,4,2048]{2,1,0:T(4,128)(2,1)} %param.12) | copy-start | bytes 49156
  119.2 74.5 %collective-permute-start.5 = (f32[2,4,8,2]{1,3,2,0:T(2,128)S(1)}, f32[2,4,8,2]{1,3,2,0:T(2,128)S(1)}, u32[]{:S(2)}, u32[]{:S(2)}) collective-permute-start(f32[2,4,8,2]{1,3,2,0:T(2,128)S(1)} %get-tuple-element.18), channel_id=1, source_target_pairs={{1,0},{2,1},{3,2},{4,3},{5,4},{6,5},{7,6},{8,7},{9,8},{10,9},{11,1... | collective-permute-start | bytes 1544 | tf_op jit(solution)/shard_map/ppermute | solution.py:20
  120.6 73.3 %collective-permute-start.4 = (f32[2,4,8,2]{1,3,2,0:T(2,128)S(1)}, f32[2,4,8,2]{1,3,2,0:T(2,128)S(1)}, u32[]{:S(2)}, u32[]{:S(2)}) collective-permute-start(f32[2,4,8,2]{1,3,2,0:T(2,128)S(1)} %get-tuple-element.18), channel_id=1, source_target_pairs={{15,0},{0,1},{1,2},{2,3},{3,4},{4,5},{5,6},{6,7},{7,8},{8,9},{9,10... | collective-permute-start | bytes 1544 | tf_op jit(solution)/shard_map/ppermute | solution.py:20
  189.2 6.4 %collective-permute-start.2 = (f32[2,4,8,2,128]{4,1,3,2,0:T(4,128)S(1)}, f32[2,4,8,2,128]{4,1,3,2,0:T(4,128)S(1)}, u32[]{:S(2)}, u32[]{:S(2)}) collective-permute-start(f32[2,4,8,2,128]{4,1,3,2,0:T(4,128)S(1)} %get-tuple-element.17), channel_id=1, source_target_pairs={{15,0},{0,1},{1,2},{2,3},{3,4},{4,5},{5,6},{6,7},{7,8},{8,9},{9,10... | collective-permute-start | bytes 196616 | tf_op jit(solution)/shard_map/ppermute | solution.py:20
  189.5 6.2 %collective-permute-start.3 = (f32[2,4,8,2,128]{4,1,3,2,0:T(4,128)S(1)}, f32[2,4,8,2,128]{4,1,3,2,0:T(4,128)S(1)}, u32[]{:S(2)}, u32[]{:S(2)}) collective-permute-start(f32[2,4,8,2,128]{4,1,3,2,0:T(4,128)S(1)} %get-tuple-element.17), channel_id=1, source_target_pairs={{1,0},{2,1},{3,2},{4,3},{5,4},{6,5},{7,6},{8,7},{9,8},{10,9},{11,1... | collective-permute-start | bytes 196616 | tf_op jit(solution)/shard_map/ppermute | solution.py:20
Sparse Core Ops, SparseCore 0:
  9.6 84.1 all-gather.4
  96.1 79.7 all-gather.2
where the time goes:
time: 204 us; the launch traced here: 203 us
  waiting for transfers between devices  131 us (64%)
  matrix products  26.2 us (13%)
  local copies, waits for them, and re-layouts  14 us (7%)
  between operations  13.5 us (7%)
  starting transfers between devices  11.5 us (6%)
  other arithmetic  7.53 us (4%)
    all_gather x1, waiting for transfers between devices, shards(): lax.all_gather(w_key, 'dev', axis=0, tiled=True)  72.5 us
    all_gather x1, waiting for transfers between devices, shards(): lax.all_gather(w_value, 'dev', axis=0, tiled=True)  55.3 us
    dot_general x1, local copies, waits for them, and re-layouts, shards(): jnp.dot(normed, lax.all_gather(w_key, 'dev', axis=0, tiled=True), preferr...  12.8 us
    dot_general x1, matrix products, shards(): jnp.dot(normed, lax.all_gather(w_value, 'dev', axis=0, tiled=True), prefe...  12.2 us
    ppermute x6, starting transfers between devices, passed_along(): return lax.ppermute(block, axis, route)  11.5 us
    dot_general x1, matrix products, shards(): jnp.dot(normed, lax.all_gather(w_key, 'dev', axis=0, tiled=True), preferr...  11.5 us
    reduce_sum x1, other arithmetic, shards(): mean_square = jnp.mean(values32 * values32, axis=-1, keepdims=True)  4.47 us
  transfers between devices with their start and end apart: 8, of which 3 were waited for; matrix products, arithmetic and copies ran while one was open for 23% of the time, Pallas kernels for 0%

commit v1 on v0

v1 whole, which is shorter than its diff:
```python
import functools

import jax
import jax.numpy as jnp
import numpy as np
from jax import lax
from jax.experimental import pallas as pl
from jax.experimental.pallas import tpu as pltpu
from jax.sharding import PartitionSpec as P

HEAD_DIM = 128
KV_HEADS = 8
Q_HEADS = 16
STEPS = 4
ROWS = STEPS * Q_HEADS

CAP_LIMIT = 50.0
QUERY_SCALE = 1.0 / 12.0
EPSILON = 1e-06

SIDE = 256
MIDDLE = 512
MESH = pl.DeviceIdType.MESH


def rotation_tables(length):
    half = HEAD_DIM // 2
    inverse = 10000.0 ** (-(np.arange(half, dtype=np.float64) * 2.0) / HEAD_DIM)
    angles = np.arange(length, dtype=np.float64)[:, None] * inverse[None, :]
    cosine, sine = np.cos(angles), np.sin(angles)
    return (
        np.concatenate([cosine, cosine], axis=1).astype(np.float32),
        np.concatenate([-sine, sine], axis=1).astype(np.float32),
    )


def softcap_exp(scores):
    return jnp.exp(CAP_LIMIT * jnp.tanh(scores * (QUERY_SCALE / CAP_LIMIT)))


def dot_t(a, b):
    return lax.dot_general(a, b, (((1,), (1,)), ((), ())), preferred_element_type=jnp.float32)


def kernel(
    snake, hidden, gain, w_key, w_value, queries, new_keys, new_values, cosines, sines, owner,
    out,
    raw, normed, weights, sums, query_rows, got_queries, fresh_rows, scores, dens, nums, sent, got, out32,
    hidden_sem, own_sem, a_send, a_recv, b_send, b_recv, x_send, x_recv,
    so_send, so_recv, sa_send, sa_recv, sb_send, sb_recv, sx_send, sx_recv,
    q_send, q_recv, r_send, r_recv,
):
    devices = lax.axis_size("dev")
    chips = devices // 2
    group = lax.axis_index("groups")
    me = lax.axis_index("dev")
    chip, core = me // 2, me % 2
    odd = group % 2
    partner = group + 1 - 2 * odd
    passages, length, width = hidden.shape
    depth = width // devices

    def chip_at(place):
        place = lax.rem(place + 2 * chips, chips)
        if not snake:
            return place
        return jnp.where(place < chips // 2, 2 * place, 2 * (chips - 1 - place) + 1)

    if snake:
        place = jnp.where(chip % 2 == 0, chip // 2, chips - 1 - chip // 2)
    else:
        place = chip

    def device_at(position, which):
        return chip_at(position) * 2 + which

    ahead, behind = device_at(place + 1, core), device_at(place - 1, core)
    sibling = chip * 2 + 1 - core
    right, left = lax.rem(me + 1, devices), lax.rem(me + devices - 1, devices)

    barrier = pltpu.get_barrier_semaphore()
    friends = [(group, ahead), (group, behind), (group, sibling), (partner, me), (group, right), (group, left)]
    for friend in friends:
        pl.semaphore_signal(barrier, inc=1, device_id=friend, device_id_type=MESH)

    loads = [
        pltpu.make_async_copy(hidden.at[p], raw.at[p], hidden_sem.at[p]) for p in range(passages)
    ]
    for load in loads:
        load.start()
    sources = (w_key, w_value)
    own_loads = [
        pltpu.make_async_copy(sources[m], weights.at[m, me], own_sem.at[m]) for m in range(2)
    ]
    for load in own_loads:
        load.start()

    side = pl.ds(pl.multiple_of(odd * (SIDE + MIDDLE), 128), SIDE)
    other_side = pl.ds(pl.multiple_of((1 - odd) * (SIDE + MIDDLE), 128), SIDE)
    middle = pl.ds(SIDE, MIDDLE)

    def remote(src, dst, send, recv, target):
        return pltpu.make_async_remote_copy(
            src_ref=src, dst_ref=dst, send_sem=send, recv_sem=recv, device_id=target, device_id_type=MESH
        )

    sign = (1, -1)
    a_target = ((group, ahead), (group, behind))
    b_target = ((group, behind), (group, ahead))

    def block(m, e, columns):
        return weights.at[m, e, :, columns]

    def a_from(m, s, which):
        return device_at(place - sign[m] * s, which)

    def b_from(m, s, which):
        return device_at(place + sign[m] * s, which)

    def send_a(m, s):
        e = a_from(m, s - 1, core)
        ref = block(m, e, side)
        return remote(ref, ref, a_send.at[m, s], a_recv.at[m, s], a_target[m])

    def send_b(m, s):
        e = b_from(m, s - 1, core)
        ref = block(m, e, middle)
        return remote(ref, ref, b_send.at[m, s], b_recv.at[m, s], b_target[m])

    def recv_a(m, s):
        ref = block(m, a_from(m, s, core), side)
        return remote(ref, ref, a_send.at[m, s], a_recv.at[m, s], a_target[m])

    def recv_b(m, s):
        ref = block(m, b_from(m, s, core), middle)
        return remote(ref, ref, b_send.at[m, s], b_recv.at[m, s], b_target[m])

    def send_x(m, s):
        ref = block(m, a_from(m, s, core), side)
        return remote(ref, ref, x_send.at[m, s], x_recv.at[m, s], (partner, me))

    def recv_x(m, s):
        ref = block(m, a_from(m, s, core), other_side)
        return remote(ref, ref, x_send.at[m, s], x_recv.at[m, s], (partner, me))

    def share(m, s, kind, which):
        columns, origin, send, recv = {
            "a": (side, a_from, sa_send, sa_recv),
            "b": (middle, b_from, sb_send, sb_recv),
            "x": (other_side, a_from, sx_send, sx_recv),
        }[kind]
        ref = block(m, origin(m, s, which), columns)
        return remote(ref, ref, send.at[m, s], recv.at[m, s], (group, sibling))

    def first_a(m):
        return remote(
            sources[m].at[:, side], block(m, me, side), a_send.at[m, 1], a_recv.at[m, 1], a_target[m]
        )

    def first_b(m):
        return remote(
            sources[m].at[:, middle], block(m, me, middle), b_send.at[m, 1], b_recv.at[m, 1], b_target[m]
        )

    def share_own(m, e):
        return remote(sources[m], weights.at[m, e], so_send.at[m], so_recv.at[m], (group, sibling))

    def send_queries(slot, target):
        return remote(query_rows, got_queries.at[slot], q_send.at[slot], q_recv.at[slot], (group, target))

    pl.semaphore_wait(barrier, len(friends))
    for m in range(2):
        first_a(m).start()
        first_b(m).start()
    for m in range(2):
        share_own(m, me).start()

    all_queries = queries[...].astype(jnp.float32)
    for h in range(Q_HEADS):
        query_rows[pl.ds(h * STEPS, STEPS), :] = all_queries[:, h * HEAD_DIM : (h + 1) * HEAD_DIM]
    send_queries(0, left).start()
    send_queries(1, right).start()

    gains = gain[...].astype(jnp.float32)
    tile = 16

    for p in range(passages):
        loads[p].wait()

        @pl.loop(0, length // tile)
        def _(i):
            rows = pl.ds(pl.multiple_of(i * tile, tile), tile)
            x = raw[p, rows, :].astype(jnp.float32)
            scale = lax.rsqrt(jnp.mean(x * x, axis=-1, keepdims=True) + EPSILON)
            y = (x * scale * gains).astype(jnp.bfloat16)
            to = pl.ds(pl.multiple_of(p * length + i * tile, tile), tile)
            for e in range(devices):
                normed[e, to, :] = y[:, e * depth : (e + 1) * depth]

    def gemm(m, e0, e1, start, count, init=False):
        @pl.loop(0, count)
        def _(j):
            columns = pl.ds(pl.multiple_of(start + j * 256, 256), 256)
            part = jnp.dot(normed[e0], weights[m, e0, :, columns], preferred_element_type=jnp.float32)
            part += jnp.dot(normed[e1], weights[m, e1, :, columns], preferred_element_type=jnp.float32)
            if init:
                sums[m, :, columns] = part
            else:
                sums[m, :, columns] += part

    def ring(m, s):
        recv_a(m, s).wait_recv()

        @pl.when(s < chips - 1)
        def _():
            send_a(m, s + 1).start()

        send_x(m, s).start()
        share(m, s, "a", core).start()
        recv_b(m, s).wait_recv()

        @pl.when(s < chips - 1)
        def _():
            send_b(m, s + 1).start()

        share(m, s, "b", core).start()

    def cross(m, s):
        recv_x(m, s).wait_recv()
        share(m, s, "x", core).start()

    def compute_ab(m, s):
        share(m, s, "a", 1 - core).wait_recv()
        share(m, s, "b", 1 - core).wait_recv()
        gemm(m, a_from(m, s, 0), a_from(m, s, 1), odd * (SIDE + MIDDLE), SIDE // 256)
        gemm(m, b_from(m, s, 0), b_from(m, s, 1), SIDE, MIDDLE // 256)

    def compute_x(m, s):
        share(m, s, "x", 1 - core).wait_recv()
        gemm(m, a_from(m, s, 0), a_from(m, s, 1), (1 - odd) * (SIDE + MIDDLE), SIDE // 256)

    last = chips - 1
    ring(0, 1)
    for m in range(2):
        own_loads[m].wait()
        share_own(m, sibling).wait_recv()
        gemm(m, chip * 2, chip * 2 + 1, 0, (2 * SIDE + MIDDLE) // 256, init=True)

    def step(i):
        ring(0, i)
        ring(1, i - 1)
        cross(0, i - 1)
        compute_ab(0, i - 1)

        @pl.when(i >= 3)
        def _():
            cross(1, i - 2)
            compute_ab(1, i - 2)
            compute_x(0, i - 2)

        @pl.when(i >= 4)
        def _():
            compute_x(1, i - 3)

    pl.loop(2, chips)(step)

    ring(1, last)
    cross(0, last)
    cross(1, last - 1)
    compute_ab(0, last)
    compute_x(0, last - 1)
    cross(1, last)
    compute_x(0, last)

    for slot, source in ((0, right), (1, left)):
        send_queries(slot, source).wait_recv()
    for p in range(passages):
        owned_by = owner[me * passages + p]
        from_self = jnp.where(owned_by == me, 1.0, 0.0)
        from_right = jnp.where(owned_by == right, 1.0, 0.0)
        from_left = jnp.where(owned_by == left, 1.0, 0.0)
        chosen = query_rows[...] * from_self + got_queries[0] * from_right + got_queries[1] * from_left
        chosen = chosen.astype(jnp.bfloat16)
        rows = pl.ds(p * length, length)
        for g in range(KV_HEADS):
            k = sums[0, rows, g * HEAD_DIM : (g + 1) * HEAD_DIM]
            turned = k * cosines[...] + pltpu.roll(k, HEAD_DIM // 2, 1) * sines[...]
            scores[p, g * 8 : (g + 1) * 8, :] = dot_t(
                chosen[g * 8 : (g + 1) * 8, :], turned.astype(jnp.bfloat16)
            )
        w = softcap_exp(scores[p])
        dens[p] = jnp.broadcast_to(jnp.sum(w, axis=-1, keepdims=True), (ROWS, HEAD_DIM))
        scores[p] = w

    all_keys = new_keys[...].astype(jnp.float32)
    all_values = new_values[...].astype(jnp.float32)
    for g in range(KV_HEADS):
        fresh_rows[0, pl.ds(g * STEPS, STEPS), :] = all_keys[:, g * HEAD_DIM : (g + 1) * HEAD_DIM]
        fresh_rows[1, pl.ds(g * STEPS, STEPS), :] = all_values[:, g * HEAD_DIM : (g + 1) * HEAD_DIM]
    fresh = dot_t(query_rows[...].astype(jnp.bfloat16), fresh_rows[0].astype(jnp.bfloat16))
    row = lax.broadcasted_iota(jnp.int32, fresh.shape, 0)
    column = lax.broadcasted_iota(jnp.int32, fresh.shape, 1)
    seen = (row // 8 == column // STEPS) & (column % STEPS <= row % STEPS)
    fresh = jnp.where(seen, softcap_exp(fresh), 0.0)
    fresh_den = jnp.broadcast_to(jnp.sum(fresh, axis=-1, keepdims=True), (ROWS, HEAD_DIM))
    fresh_num = jnp.dot(
        fresh.astype(jnp.bfloat16), fresh_rows[1].astype(jnp.bfloat16), preferred_element_type=jnp.float32
    )

    compute_ab(1, last - 1)
    compute_x(1, last - 2)
    compute_x(1, last - 1)
    compute_ab(1, last)
    compute_x(1, last)

    for p in range(passages):
        rows = pl.ds(p * length, length)
        w = scores[p].astype(jnp.bfloat16)
        for g in range(KV_HEADS):
            v = sums[1, rows, g * HEAD_DIM : (g + 1) * HEAD_DIM].astype(jnp.bfloat16)
            nums[p, g * 8 : (g + 1) * 8, :] = jnp.dot(
                w[g * 8 : (g + 1) * 8, :], v, preferred_element_type=jnp.float32
            )

    def picked(target):
        num = jnp.zeros((ROWS, HEAD_DIM), jnp.float32)
        den = num
        for p in range(passages):
            flag = jnp.where(owner[me * passages + p] == target, 1.0, 0.0)
            num += nums[p] * flag
            den += dens[p] * flag
        return num, den

    replies = []
    for slot, target in ((0, left), (1, right)):
        num, den = picked(target)
        sent[slot, 0] = num
        sent[slot, 1] = den
        reply = remote(sent.at[slot], got.at[slot], r_send.at[slot], r_recv.at[slot], (group, target))
        reply.start()
        replies.append(reply)
    num, den = picked(me)
    num, den = num + fresh_num, den + fresh_den
    for slot in range(2):
        replies[slot].wait_recv()
        num, den = num + got[slot, 0], den + got[slot, 1]
    result = num / den
    for h in range(Q_HEADS):
        out32[:, h * HEAD_DIM : (h + 1) * HEAD_DIM] = result[h * STEPS : (h + 1) * STEPS, :]
    out[...] = out32[...].astype(jnp.bfloat16)

    for reply in replies:
        reply.wait_send()
    for slot, target in ((0, left), (1, right)):
        send_queries(slot, target).wait_send()
    for m in range(2):
        share_own(m, me).wait_send()
        first_a(m).wait_send()
        first_b(m).wait_send()

    @pl.loop(1, chips)
    def _(s):
        for m in range(2):
            send_x(m, s).wait_send()
            for kind in "abx":
                share(m, s, kind, core).wait_send()

    @pl.loop(2, chips)
    def _(s):
        for m in range(2):
            send_a(m, s).wait_send()
            send_b(m, s).wait_send()


def shards(snake, hidden, norm_gain, w_key, w_value, queries, new_keys, new_values, passage_owner):
    passages, length, width = hidden.shape
    depth, columns = w_key.shape
    devices = lax.axis_size("dev")
    chips = devices // 2
    tokens = passages * length
    cosines, sines = rotation_tables(length)
    vmem = pl.BlockSpec(memory_space=pltpu.VMEM)
    hbm = pl.BlockSpec(memory_space=pl.ANY)
    pair = pltpu.SemaphoreType.DMA((2,))
    staged = pltpu.SemaphoreType.DMA((2, chips))
    f32 = jnp.float32
    out = pl.pallas_call(
        functools.partial(kernel, snake),
        out_shape=jax.ShapeDtypeStruct((STEPS, Q_HEADS * HEAD_DIM), jnp.bfloat16),
        in_specs=[hbm, vmem, hbm, hbm, vmem, vmem, vmem, vmem, vmem, pl.BlockSpec(memory_space=pltpu.SMEM)],
        out_specs=vmem,
        scratch_shapes=[
            pltpu.VMEM((passages, length, width), jnp.bfloat16),
            pltpu.VMEM((devices, tokens, depth), jnp.bfloat16),
            pltpu.VMEM((2, devices, depth, columns), jnp.bfloat16),
            pltpu.VMEM((2, tokens, columns), f32),
            pltpu.VMEM((ROWS, HEAD_DIM), f32),
            pltpu.VMEM((2, ROWS, HEAD_DIM), f32),
            pltpu.VMEM((2, STEPS * KV_HEADS, HEAD_DIM), f32),
            pltpu.VMEM((passages, ROWS, length), f32),
            pltpu.VMEM((passages, ROWS, HEAD_DIM), f32),
            pltpu.VMEM((passages, ROWS, HEAD_DIM), f32),
            pltpu.VMEM((2, 2, ROWS, HEAD_DIM), f32),
            pltpu.VMEM((2, 2, ROWS, HEAD_DIM), f32),
            pltpu.VMEM((STEPS, Q_HEADS * HEAD_DIM), f32),
            pltpu.SemaphoreType.DMA((passages,)),
            pair,
            *[staged] * 6,
            pair,
            pair,
            *[staged] * 6,
            *[pair] * 4,
        ],
        compiler_params=pltpu.CompilerParams(
            collective_id=0, has_side_effects=True, vmem_limit_bytes=58 * 2**20
        ),
        cost_estimate=pl.CostEstimate(
            flops=4 * tokens * width * columns, bytes_accessed=2 * tokens * width, transcendentals=0
        ),
    )(
        hidden,
        norm_gain.reshape(1, width),
        w_key,
        w_value,
        queries[0],
        new_keys[0],
        new_values[0],
        cosines,
        sines,
        passage_owner,
    )
    return out[None]


def solution(mesh):
    snake = mesh.shape["groups"] == 2
    return jax.shard_map(
        functools.partial(shards, snake),
        mesh=mesh,
        in_specs=(
            P(("groups", "dev"), None, None),
            P(),
            P("dev", None),
            P("dev", None),
            P(("groups", "dev"), None, None),
            P(("groups", "dev"), None, None),
            P(("groups", "dev"), None, None),
            P("groups"),
        ),
        out_specs=P(("groups", "dev"), None, None),
        check_vma=False,
    )
```

time: 204 us -> 103 us (0.50)
  waiting for transfers between devices: 131 us -> 0 us
  Pallas kernels: 0 us -> 100 us
  matrix products: 26.2 us -> 0 us
  between operations: 13.5 us -> 0.01 us
  starting transfers between devices: 11.5 us -> 0 us
  local copies, waits for them, and re-layouts: 14 us -> 2.64 us
  other arithmetic: 7.53 us -> 0 us
    all_gather x2 -> x0, waiting for transfers between devices: 128 us -> none  [the longest x1 72.5 us: shards(): lax.all_gather(w_key, 'dev', axis=0, tiled=True)]
    pallas_call x0 -> x1, Pallas kernels: none -> 100 us  [shards(): pl.pallas_call(functools.partial(kernel, snake), out_shape=jax.ShapeDtype...]
    dot_general x6 -> x0, matrix products: 26.2 us -> none  [the longest x1 12.2 us: shards(): jnp.dot(normed, lax.all_gather(w_value, 'dev', axis=0, tiled=True), prefe...]
    dot_general x2 -> x0, local copies, waits for them, and re-layouts: 12.9 us -> none  [the longest x1 12.8 us: shards(): jnp.dot(normed, lax.all_gather(w_key, 'dev', axis=0, tiled=True), preferr...]
    ppermute x6 -> x0, starting transfers between devices: 11.5 us -> none  [passed_along(): return lax.ppermute(block, axis, route)]
    reduce_sum x7 -> x0, other arithmetic: 5.01 us -> none  [the longest x1 4.47 us: shards(): mean_square = jnp.mean(values32 * values32, axis=-1, keepdims=True)]
  transfers between devices with their start and end apart: 8 -> 0, of which waited for: 3 -> 0; matrix products, arithmetic and copies ran while one was open for 23% -> 0% of each run, Pallas kernels for 0% -> 0%
where the time goes in v1:
time: 103 us
  Pallas kernels  100 us (97%)
  local copies, waits for them, and re-layouts  2.64 us (3%)
    pallas_call x1, Pallas kernels, shards(): pl.pallas_call(functools.partial(kernel, snake), out_shape=jax.ShapeDtype...  100 us

profile of v1, /device:TPU:0, one launch (start us, length us, event | category | flops | bytes accessed | tf_op | source)
XLA Modules:
  0.0 102.8 jit_solution(11922130659290295236)
XLA Ops:
  0.0 1.3 %reshape.3.gain = bf16[1,4608]{1,0:T(2,128)(2,1)} reshape(bf16[4608]{0:T(1024)(128)(2,1)} %param.11) | data formatting | bytes 18432 | tf_op jit(solution)/shard_map/reshape | solution.py:422
  1.3 100.1 %shard_map.100 = bf16[4,2048]{1,0:T(4,128)(2,1)} custom-call(bf16[2,384,4608]{2,1,0:T(8,128)(2,1)} %hidden.1, bf16[1,4608]{1,0:T(2,128)(2,1)} %reshape.3.gain, bf16[288,1024]{1,0:T(8,128)(2,1)} %w_key.1, bf16[288,1024]{1,0:T(8,128)(2,1)} %w_value.1, bf16[4,2048]{1,0:T(4,128)(2,1)} %bitcast.5, bf16[4,1024]{1,0:T(4,128)(2,1)} %bitcast.6, ...), custom_call_target="tpu_custom_call" | custom-call | flops 14495514624 | bytes 7077888 | tf_op jit(solution)/shard_map/pallas_call | solution.py:387
  101.4 1.3 %copy.12 = bf16[1,4,2048]{2,1,0:T(4,128)(2,1)} copy(bf16[1,4,2048]{2,1,0:T(4,128)(2,1)} %bitcast.4) | data formatting | bytes 32768

commit v2 on v1

--- a/solution.py
+++ b/solution.py
@@ -18,8 +18,15 @@
 QUERY_SCALE = 1.0 / 12.0
 EPSILON = 1e-06
 
-SIDE = 256
-MIDDLE = 512
+SIDE = (256, 384)
+MIDDLE = (512, 256)
+SHIFT = (768, 640)
+STREAMS = (
+    (0, 0, 128, 256, 256),
+    (0, 128, 128, 512, 256),
+    (1, 0, 128, 384, 128),
+    (1, 128, 256, 512, 128),
+)
 MESH = pl.DeviceIdType.MESH
 
 
@@ -95,72 +102,74 @@
     for load in own_loads:
         load.start()
 
-    side = pl.ds(pl.multiple_of(odd * (SIDE + MIDDLE), 128), SIDE)
-    other_side = pl.ds(pl.multiple_of((1 - odd) * (SIDE + MIDDLE), 128), SIDE)
-    middle = pl.ds(SIDE, MIDDLE)
+    def side(k):
+        m, start, size, _, _ = STREAMS[k]
+        return pl.ds(pl.multiple_of(start + odd * SHIFT[m], 128), size)
+
+    def other_side(k):
+        m, start, size, _, _ = STREAMS[k]
+        return pl.ds(pl.multiple_of(start + (1 - odd) * SHIFT[m], 128), size)
+
+    def middle(k):
+        return pl.ds(STREAMS[k][3], STREAMS[k][4])
 
     def remote(src, dst, send, recv, target):
         return pltpu.make_async_remote_copy(
             src_ref=src, dst_ref=dst, send_sem=send, recv_sem=recv, device_id=target, device_id_type=MESH
         )
 
-    sign = (1, -1)
-    a_target = ((group, ahead), (group, behind))
-    b_target = ((group, behind), (group, ahead))
-
-    def block(m, e, columns):
-        return weights.at[m, e, :, columns]
-
-    def a_from(m, s, which):
-        return device_at(place - sign[m] * s, which)
-
-    def b_from(m, s, which):
-        return device_at(place + sign[m] * s, which)
-
-    def send_a(m, s):
-        e = a_from(m, s - 1, core)
-        ref = block(m, e, side)
-        return remote(ref, ref, a_send.at[m, s], a_recv.at[m, s], a_target[m])
-
-    def send_b(m, s):
-        e = b_from(m, s - 1, core)
-        ref = block(m, e, middle)
-        return remote(ref, ref, b_send.at[m, s], b_recv.at[m, s], b_target[m])
-
-    def recv_a(m, s):
-        ref = block(m, a_from(m, s, core), side)
-        return remote(ref, ref, a_send.at[m, s], a_recv.at[m, s], a_target[m])
-
-    def recv_b(m, s):
-        ref = block(m, b_from(m, s, core), middle)
-        return remote(ref, ref, b_send.at[m, s], b_recv.at[m, s], b_target[m])
-
-    def send_x(m, s):
-        ref = block(m, a_from(m, s, core), side)
-        return remote(ref, ref, x_send.at[m, s], x_recv.at[m, s], (partner, me))
-
-    def recv_x(m, s):
-        ref = block(m, a_from(m, s, core), other_side)
-        return remote(ref, ref, x_send.at[m, s], x_recv.at[m, s], (partner, me))
-
-    def share(m, s, kind, which):
+    a_target = (group, jnp.where(core == 0, ahead, behind))
+    b_target = (group, jnp.where(core == 0, behind, ahead))
+
+    def block(k, e, columns):
+        return weights.at[STREAMS[k][0], e, :, columns]
+
+    def a_from(s, which):
+        return device_at(place - (1 - 2 * which) * s, which)
+
+    def b_from(s, which):
+        return device_at(place + (1 - 2 * which) * s, which)
+
+    def send_a(k, s):
+        ref = block(k, a_from(s - 1, core), side(k))
+        return remote(ref, ref, a_send.at[k, s], a_recv.at[k, s], a_target)
+
+    def send_b(k, s):
+        ref = block(k, b_from(s - 1, core), middle(k))
+        return remote(ref, ref, b_send.at[k, s], b_recv.at[k, s], b_target)
+
+    def recv_a(k, s):
+        ref = block(k, a_from(s, core), side(k))
+        return remote(ref, ref, a_send.at[k, s], a_recv.at[k, s], a_target)
+
+    def recv_b(k, s):
+        ref = block(k, b_from(s, core), middle(k))
+        return remote(ref, ref, b_send.at[k, s], b_recv.at[k, s], b_target)
+
+    def send_x(k, s):
+        ref = block(k, a_from(s, core), side(k))
+        return remote(ref, ref, x_send.at[k, s], x_recv.at[k, s], (partner, me))
+
+    def recv_x(k, s):
+        ref = block(k, a_from(s, core), other_side(k))
+        return remote(ref, ref, x_send.at[k, s], x_recv.at[k, s], (partner, me))
+
+    def share(k, s, kind, which):
         columns, origin, send, recv = {
             "a": (side, a_from, sa_send, sa_recv),
             "b": (middle, b_from, sb_send, sb_recv),
             "x": (other_side, a_from, sx_send, sx_recv),
         }[kind]
-        ref = block(m, origin(m, s, which), columns)
-        return remote(ref, ref, send.at[m, s], recv.at[m, s], (group, sibling))
-
-    def first_a(m):
-        return remote(
-            sources[m].at[:, side], block(m, me, side), a_send.at[m, 1], a_recv.at[m, 1], a_target[m]
-        )
-
-    def first_b(m):
-        return remote(
-            sources[m].at[:, middle], block(m, me, middle), b_send.at[m, 1], b_recv.at[m, 1], b_target[m]
-        )
+        ref = block(k, origin(s, which), columns(k))
+        return remote(ref, ref, send.at[k, s], recv.at[k, s], (group, sibling))
+
+    def first_a(k):
+        source = sources[STREAMS[k][0]].at[:, side(k)]
+        return remote(source, block(k, me, side(k)), a_send.at[k, 1], a_recv.at[k, 1], a_target)
+
+    def first_b(k):
+        source = sources[STREAMS[k][0]].at[:, middle(k)]
+        return remote(source, block(k, me, middle(k)), b_send.at[k, 1], b_recv.at[k, 1], b_target)
 
     def share_own(m, e):
         return remote(sources[m], weights.at[m, e], so_send.at[m], so_recv.at[m], (group, sibling))
@@ -169,11 +178,13 @@
         return remote(query_rows, got_queries.at[slot], q_send.at[slot], q_recv.at[slot], (group, target))
 
     pl.semaphore_wait(barrier, len(friends))
-    for m in range(2):
-        first_a(m).start()
-        first_b(m).start()
-    for m in range(2):
+    def first(m):
+        for k in (2 * m, 2 * m + 1):
+            first_a(k).start()
+            first_b(k).start()
         share_own(m, me).start()
+
+    first(0)
 
     all_queries = queries[...].astype(jnp.float32)
     for h in range(Q_HEADS):
@@ -181,13 +192,11 @@
     send_queries(0, left).start()
     send_queries(1, right).start()
 
-    gains = gain[...].astype(jnp.float32)
+    gains = gain[...].astype(jnp.float32)[None, :]
     tile = 16
 
-    for p in range(passages):
-        loads[p].wait()
-
-        @pl.loop(0, length // tile)
+    def normalize(p, begin, end):
+        @pl.loop(begin // tile, end // tile)
         def _(i):
             rows = pl.ds(pl.multiple_of(i * tile, tile), tile)
             x = raw[p, rows, :].astype(jnp.float32)
@@ -197,10 +206,12 @@
             for e in range(devices):
                 normed[e, to, :] = y[:, e * depth : (e + 1) * depth]
 
-    def gemm(m, e0, e1, start, count, init=False):
-        @pl.loop(0, count)
+    def gemm(m, e0, e1, start, width, init=False):
+        size = width if width < 512 else 256
+
+        @pl.loop(0, width // size)
         def _(j):
-            columns = pl.ds(pl.multiple_of(start + j * 256, 256), 256)
+            columns = pl.ds(pl.multiple_of(start + j * size, 128), size)
             part = jnp.dot(normed[e0], weights[m, e0, :, columns], preferred_element_type=jnp.float32)
             part += jnp.dot(normed[e1], weights[m, e1, :, columns], preferred_element_type=jnp.float32)
             if init:
@@ -208,73 +219,100 @@
             else:
                 sums[m, :, columns] += part
 
-    def ring(m, s):
-        recv_a(m, s).wait_recv()
+    def ring(k, s):
+        recv_a(k, s).wait_recv()
 
         @pl.when(s < chips - 1)
         def _():
-            send_a(m, s + 1).start()
-
-        send_x(m, s).start()
-        share(m, s, "a", core).start()
-        recv_b(m, s).wait_recv()
+            send_a(k, s + 1).start()
+
+        send_x(k, s).start()
+        share(k, s, "a", core).start()
+        recv_b(k, s).wait_recv()
 
         @pl.when(s < chips - 1)
         def _():
-            send_b(m, s + 1).start()
-
-        share(m, s, "b", core).start()
+            send_b(k, s + 1).start()
+
+        share(k, s, "b", core).start()
 
     def cross(m, s):
-        recv_x(m, s).wait_recv()
-        share(m, s, "x", core).start()
-
-    def compute_ab(m, s):
-        share(m, s, "a", 1 - core).wait_recv()
-        share(m, s, "b", 1 - core).wait_recv()
-        gemm(m, a_from(m, s, 0), a_from(m, s, 1), odd * (SIDE + MIDDLE), SIDE // 256)
-        gemm(m, b_from(m, s, 0), b_from(m, s, 1), SIDE, MIDDLE // 256)
-
-    def compute_x(m, s):
-        share(m, s, "x", 1 - core).wait_recv()
-        gemm(m, a_from(m, s, 0), a_from(m, s, 1), (1 - odd) * (SIDE + MIDDLE), SIDE // 256)
+        for k in (2 * m, 2 * m + 1):
+            recv_x(k, s).wait_recv()
+            share(k, s, "x", core).start()
+
+    def compute(m, s, kind):
+        for k in (2 * m, 2 * m + 1):
+            share(k, s, kind, 1 - core).wait_recv()
+        if kind == "b":
+            gemm(m, b_from(s, 0), b_from(s, 1), SIDE[m], MIDDLE[m])
+        else:
+            start = (odd if kind == "a" else 1 - odd) * SHIFT[m]
+            gemm(m, a_from(s, 0), a_from(s, 1), start, SIDE[m])
 
     last = chips - 1
-    ring(0, 1)
+    split = length // 2 // tile * tile
+    loads[0].wait()
+    normalize(0, 0, split)
+    first(1)
+    normalize(0, split, length)
+    for p in range(1, passages):
+        loads[p].wait()
+        if p == 1:
+            ring(0, 1)
+        normalize(p, 0, split)
+        if p == 1:
+            ring(1, 1)
+        normalize(p, split, length)
     for m in range(2):
         own_loads[m].wait()
         share_own(m, sibling).wait_recv()
-        gemm(m, chip * 2, chip * 2 + 1, 0, (2 * SIDE + MIDDLE) // 256, init=True)
+        gemm(m, chip * 2, chip * 2 + 1, 0, 2 * SIDE[m] + MIDDLE[m], init=True)
 
     def step(i):
         ring(0, i)
-        ring(1, i - 1)
+        compute(0, i - 1, "b")
+        ring(2, i - 1)
         cross(0, i - 1)
-        compute_ab(0, i - 1)
 
         @pl.when(i >= 3)
         def _():
+            compute(1, i - 2, "a")
+
+        ring(1, i)
+        compute(0, i - 1, "a")
+
+        @pl.when(i >= 3)
+        def _():
+            compute(0, i - 2, "x")
+
+        ring(3, i - 1)
+
+        @pl.when(i >= 3)
+        def _():
             cross(1, i - 2)
-            compute_ab(1, i - 2)
-            compute_x(0, i - 2)
+            compute(1, i - 2, "b")
 
         @pl.when(i >= 4)
         def _():
-            compute_x(1, i - 3)
+            compute(1, i - 3, "x")
 
     pl.loop(2, chips)(step)
 
-    ring(1, last)
+    ring(2, last)
     cross(0, last)
+    compute(0, last, "b")
+    ring(3, last)
     cross(1, last - 1)
-    compute_ab(0, last)
-    compute_x(0, last - 1)
-    cross(1, last)
-    compute_x(0, last)
+    compute(0, last, "a")
+    compute(0, last - 1, "x")
+    compute(0, last, "x")
 
     for slot, source in ((0, right), (1, left)):
         send_queries(slot, source).wait_recv()
     for p in range(passages):
+        if p == 1:
+            cross(1, last)
         owned_by = owner[me * passages + p]
         from_self = jnp.where(owned_by == me, 1.0, 0.0)
         from_right = jnp.where(owned_by == right, 1.0, 0.0)
@@ -307,11 +345,13 @@
         fresh.astype(jnp.bfloat16), fresh_rows[1].astype(jnp.bfloat16), preferred_element_type=jnp.float32
     )
 
-    compute_ab(1, last - 1)
-    compute_x(1, last - 2)
-    compute_x(1, last - 1)
-    compute_ab(1, last)
-    compute_x(1, last)
+    compute(1, last - 1, "a")
+    compute(1, last - 1, "b")
+    compute(1, last - 2, "x")
+    compute(1, last - 1, "x")
+    compute(1, last, "a")
+    compute(1, last, "b")
+    compute(1, last, "x")
 
     for p in range(passages):
         rows = pl.ds(p * length, length)
@@ -355,21 +395,22 @@
         send_queries(slot, target).wait_send()
     for m in range(2):
         share_own(m, me).wait_send()
-        first_a(m).wait_send()
-        first_b(m).wait_send()
+    for k in range(len(STREAMS)):
+        first_a(k).wait_send()
+        first_b(k).wait_send()
 
     @pl.loop(1, chips)
     def _(s):
-        for m in range(2):
-            send_x(m, s).wait_send()
+        for k in range(len(STREAMS)):
+            send_x(k, s).wait_send()
             for kind in "abx":
-                share(m, s, kind, core).wait_send()
+                share(k, s, kind, core).wait_send()
 
     @pl.loop(2, chips)
     def _(s):
-        for m in range(2):
-            send_a(m, s).wait_send()
-            send_b(m, s).wait_send()
+        for k in range(len(STREAMS)):
+            send_a(k, s).wait_send()
+            send_b(k, s).wait_send()
 
 
 def shards(snake, hidden, norm_gain, w_key, w_value, queries, new_keys, new_values, passage_owner):
@@ -382,7 +423,7 @@
     vmem = pl.BlockSpec(memory_space=pltpu.VMEM)
     hbm = pl.BlockSpec(memory_space=pl.ANY)
     pair = pltpu.SemaphoreType.DMA((2,))
-    staged = pltpu.SemaphoreType.DMA((2, chips))
+    staged = pltpu.SemaphoreType.DMA((len(STREAMS), chips))
     f32 = jnp.float32
     out = pl.pallas_call(
         functools.partial(kernel, snake),
@@ -419,7 +460,7 @@
         ),
     )(
         hidden,
-        norm_gain.reshape(1, width),
+        norm_gain,
         w_key,
         w_value,
         queries[0],

time: 103 us -> 96.7 us (0.939)
  Pallas kernels: 100 us -> 95 us
  local copies, waits for them, and re-layouts: 2.64 us -> 1.33 us
    pallas_call x1, Pallas kernels: 100 us -> 95 us  [shards(): pl.pallas_call(functools.partial(kernel, snake), out_shape=jax.ShapeDtype...]
    reshape x1 -> x0, local copies, waits for them, and re-layouts: 1.31 us -> none  [shards(): norm_gain.reshape(1, width)]
where the time goes in v2:
time: 96.7 us; the launch traced here: 96.3 us
  Pallas kernels  95 us (98%)
  local copies, waits for them, and re-layouts  1.33 us (1%)
    pallas_call x1, Pallas kernels, shards(): pl.pallas_call(functools.partial(kernel, snake), out_shape=jax.ShapeDtype...  95 us

profile of v2, /device:TPU:0, one launch (start us, length us, event | category | flops | bytes accessed | tf_op | source)
XLA Modules:
  0.0 96.3 jit_solution(8312612156684517386)
XLA Ops:
  0.0 95.0 %shard_map.100 = bf16[4,2048]{1,0:T(4,128)(2,1)} custom-call(bf16[2,384,4608]{2,1,0:T(8,128)(2,1)} %hidden.1, bf16[4608]{0:T(1024)(128)(2,1)} %gain.1, bf16[288,1024]{1,0:T(8,128)(2,1)} %w_key.1, bf16[288,1024]{1,0:T(8,128)(2,1)} %w_value.1, bf16[4,2048]{1,0:T(4,128)(2,1)} %bitcast.5, bf16[4,1024]{1,0:T(4,128)(2,1)} %bitcast.6, bf16[4,1024]{1,0:T(4,128)(2,1)} %bitcast.7, ...), custom_call_target="tpu_custom_call" | custom-call | flops 14495514624 | bytes 7077888 | tf_op jit(solution)/shard_map/pallas_call | solution.py:428
  95.0 1.3 %copy.12 = bf16[1,4,2048]{2,1,0:T(4,128)(2,1)} copy(bf16[1,4,2048]{2,1,0:T(4,128)(2,1)} %bitcast.4) | data formatting | bytes 32768
